TPU v7x, 32 devices: a whole 2x2x4 slice. The times are simulated.
32 devices in a mesh: seq: 8 (over z, x), head: 4 (over y, core).
Axes of the slice: x: 2, y: 2, z: 4, core: 2. Of those that a mesh axis runs over, the one named last changes fastest.
Arguments:
- queries: bfloat16 [2048, 2048], P('seq', 'head'), may hold values from -180 to 180
- keys: bfloat16 [2048, 2048], P('seq', 'head'), may hold values from -7 to 7
- values: bfloat16 [2048, 2048], P('seq', 'head'), may hold values from -6 to 6
- out_grad: bfloat16 [2048, 2048], P('seq', 'head'), may hold values from -6 to 6
- rand_blocks: int32 [32, 3], replicated, may hold values from 0 to 31, as said below
- glob_blocks: int32 [8], P('seq'), may hold values from 0 to 31, as said below
Outputs:
- attn_out: bfloat16 [2048, 2048], P('seq', 'head')
- query_grad: bfloat16 [2048, 2048], P('seq', 'head')
- key_grad: bfloat16 [2048, 2048], P('seq', 'head')
- value_grad: bfloat16 [2048, 2048], P('seq', 'head')
Inputs may be any that keep to these rules, and one draw needn't show every extreme that they name: `rand_blocks`: rows 4 * i to 4 * (i + 1) - 1 are the query blocks of index i of seq. Among their 12 entries, the blocks of any one index j of seq (blocks 4 * j to 4 * (j + 1) - 1) are named at most 2 times; in every draw one index j is named exactly 2 times by the rows of every index i. `glob_blocks`: entry j is one of the blocks 4 * j to 4 * (j + 1) - 1.
All inputs are finite; a program needn't handle non-finite values.
Results may differ from a plain program's by a relative error of at most 0.0052.
Values may be sent and summed in bfloat16 or wider, within the bound.
A program may use at most 128 MiB of HBM per device.

v0:
```python
import math

import jax
import jax.numpy as jnp
from jax import lax
from jax.sharding import PartitionSpec as P

HDIM = 128
BLK = 64
GLEN = 16


def extended(array, sides, width):
    for axis, dim in sides:
        size, length = (lax.axis_size(axis), array.shape[dim])
        up = [(i, (i + 1) % size) for i in range(size - 1)]
        down = [(j, i) for i, j in up]
        last = lax.slice_in_dim(array, length - width, length, axis=dim)
        first = lax.slice_in_dim(array, 0, width, axis=dim)
        before = lax.ppermute(last, axis, up)
        after = lax.ppermute(first, axis, down)
        array = jnp.concatenate([before, array, after], axis=dim)
    return array


def shards(queries, keys, values, out_grad, rand_blocks, glob_blocks):
    rows_dev, width_dev = queries.shape
    head_count = width_dev // HDIM
    seq_count = lax.axis_size("seq")
    my_index = lax.axis_index("seq")
    blocks_dev = rows_dev // BLK
    total_blocks = blocks_dev * seq_count
    per_block = rand_blocks.shape[1]
    spots = blocks_dev * per_block
    capacity = max(2, (spots + seq_count - 1) // seq_count)
    scale = 1.0 / math.sqrt(HDIM)
    local_len = (3 + per_block) * BLK
    global_len = seq_count * GLEN
    paired = jnp.stack([keys, values], 1)
    padded = extended(paired, (("seq", 0),), BLK)
    earlier = padded[:rows_dev].reshape(blocks_dev, BLK, 2, width_dev)
    current = paired.reshape(blocks_dev, BLK, 2, width_dev)
    later = padded[2 * BLK :].reshape(blocks_dev, BLK, 2, width_dev)
    own_global = glob_blocks[0] - my_index * blocks_dev
    mine = lax.dynamic_slice_in_dim(paired, own_global * BLK, GLEN, 0)
    global_kv = lax.all_gather(mine, "seq", axis=0, tiled=True)
    plan = rand_blocks.reshape(seq_count, spots)
    owners = plan // blocks_dev
    targets = plan % blocks_dev
    member = (owners[:, :, None] == jnp.arange(seq_count, dtype=jnp.int32)[None, None, :]).astype(
        jnp.int32
    )
    ranks = jnp.sum(member * (jnp.cumsum(member, axis=1) - 1), axis=2)
    places = owners * capacity + ranks
    my_places = lax.dynamic_index_in_dim(places, my_index, 0, keepdims=False)
    asked = (
        (owners == my_index)[:, :, None]
        & (ranks[:, :, None] == jnp.arange(capacity, dtype=jnp.int32)[None, None, :])
    ).astype(jnp.int32)
    incoming = jnp.sum(asked * (targets[:, :, None] + 1), axis=1) - 1
    block_kv = paired.reshape(blocks_dev, BLK, 2, width_dev)
    outgoing = jnp.take(block_kv, jnp.maximum(incoming, 0), axis=0)
    received = lax.all_to_all(outgoing, "seq", split_axis=0, concat_axis=0, tiled=True)
    fetched = jnp.take(received.reshape(seq_count * capacity, BLK, 2, width_dev), my_places, axis=0)
    fetched = fetched.reshape(blocks_dev, per_block * BLK, 2, width_dev)
    local_kv = jnp.concatenate([earlier, current, later, fetched], 1)
    query_blocks = queries.reshape(blocks_dev, BLK, head_count, HDIM)
    grad_blocks = out_grad.reshape(blocks_dev, BLK, head_count, HDIM)
    local_keys = local_kv[:, :, 0].reshape(blocks_dev, local_len, head_count, HDIM)
    local_vals = local_kv[:, :, 1].reshape(blocks_dev, local_len, head_count, HDIM)
    global_keys = global_kv[:, 0].reshape(global_len, head_count, HDIM)
    global_vals = global_kv[:, 1].reshape(global_len, head_count, HDIM)
    block_ids = my_index * blocks_dev + jnp.arange(blocks_dev, dtype=jnp.int32)
    before_ok = jnp.broadcast_to((block_ids > 0)[:, None], (blocks_dev, BLK))
    after_ok = jnp.broadcast_to((block_ids < total_blocks - 1)[:, None], (blocks_dev, BLK))
    visible = jnp.concatenate(
        [
            before_ok,
            jnp.ones((blocks_dev, BLK), bool),
            after_ok,
            jnp.ones((blocks_dev, per_block * BLK), bool),
        ],
        1,
    )
    scores_local = (
        jnp.einsum("bqhd,bkhd->bhqk", query_blocks, local_keys, preferred_element_type=jnp.float32)
        * scale
    )
    scores_local = jnp.where(visible[:, None, None, :], scores_local, -jnp.inf)
    scores_global = (
        jnp.einsum("bqhd,khd->bhqk", query_blocks, global_keys, preferred_element_type=jnp.float32)
        * scale
    )
    top = jnp.maximum(
        jnp.max(scores_local, axis=-1, keepdims=True),
        jnp.max(scores_global, axis=-1, keepdims=True),
    )
    expo_local = jnp.exp(scores_local - top)
    expo_global = jnp.exp(scores_global - top)
    totals = jnp.sum(expo_local, axis=-1, keepdims=True) + jnp.sum(
        expo_global, axis=-1, keepdims=True
    )
    probs_local = expo_local / totals
    probs_global = expo_global / totals
    weights_local = probs_local.astype(jnp.bfloat16)
    weights_global = probs_global.astype(jnp.bfloat16)
    attended = jnp.einsum(
        "bhqk,bkhd->bqhd", weights_local, local_vals, preferred_element_type=jnp.float32
    ) + jnp.einsum(
        "bhqk,khd->bqhd", weights_global, global_vals, preferred_element_type=jnp.float32
    )
    attn_out = attended.reshape(rows_dev, width_dev).astype(jnp.bfloat16)
    dprobs_local = jnp.einsum(
        "bqhd,bkhd->bhqk", grad_blocks, local_vals, preferred_element_type=jnp.float32
    )
    dprobs_global = jnp.einsum(
        "bqhd,khd->bhqk", grad_blocks, global_vals, preferred_element_type=jnp.float32
    )
    delta = jnp.sum(probs_local * dprobs_local, axis=-1, keepdims=True) + jnp.sum(
        probs_global * dprobs_global, axis=-1, keepdims=True
    )
    dscores_local = (probs_local * (dprobs_local - delta) * scale).astype(jnp.bfloat16)
    dscores_global = (probs_global * (dprobs_global - delta) * scale).astype(jnp.bfloat16)
    query_sum = jnp.einsum(
        "bhqk,bkhd->bqhd", dscores_local, local_keys, preferred_element_type=jnp.float32
    ) + jnp.einsum(
        "bhqk,khd->bqhd", dscores_global, global_keys, preferred_element_type=jnp.float32
    )
    query_grad = query_sum.reshape(rows_dev, width_dev).astype(jnp.bfloat16)
    local_dk = jnp.einsum(
        "bhqk,bqhd->bkhd", dscores_local, query_blocks, preferred_element_type=jnp.float32
    )
    local_dv = jnp.einsum(
        "bhqk,bqhd->bkhd", weights_local, grad_blocks, preferred_element_type=jnp.float32
    )
    local_grads = jnp.stack(
        [
            local_dk.reshape(blocks_dev, local_len, width_dev),
            local_dv.reshape(blocks_dev, local_len, width_dev),
        ],
        2,
    )
    before_terms = local_grads[:, :BLK].reshape(rows_dev, 2, width_dev)
    here_terms = local_grads[:, BLK : 2 * BLK].reshape(rows_dev, 2, width_dev)
    after_terms = local_grads[:, 2 * BLK : 3 * BLK].reshape(rows_dev, 2, width_dev)
    rims = jnp.concatenate([before_terms[:BLK], after_terms[rows_dev - BLK :]], 0)
    rim_padded = extended(rims.astype(jnp.bfloat16), (("seq", 0),), BLK).astype(rims.dtype)
    window_sum = (
        here_terms
        + jnp.concatenate([before_terms[BLK:], rim_padded[3 * BLK :]], 0)
        + jnp.concatenate([rim_padded[:BLK], after_terms[: rows_dev - BLK]], 0)
    )
    slot_grads = local_grads[:, 3 * BLK :].reshape(spots, BLK * 2 * width_dev).astype(jnp.bfloat16)
    placing = (
        my_places[:, None] == jnp.arange(seq_count * capacity, dtype=jnp.int32)[None, :]
    ).astype(jnp.bfloat16)
    to_send = jnp.einsum(
        "ts,tx->sx", placing, slot_grads, preferred_element_type=jnp.float32
    ).astype(jnp.bfloat16)
    returned = lax.all_to_all(
        to_send.reshape(seq_count, capacity, BLK * 2 * width_dev),
        "seq",
        split_axis=0,
        concat_axis=0,
        tiled=True,
    )
    landing = (
        incoming.reshape(-1)[:, None] == jnp.arange(blocks_dev, dtype=jnp.int32)[None, :]
    ).astype(jnp.bfloat16)
    random_sum = jnp.einsum(
        "sn,sx->nx",
        landing,
        returned.reshape(seq_count * capacity, BLK * 2 * width_dev),
        preferred_element_type=jnp.float32,
    ).reshape(rows_dev, 2, width_dev)
    global_dk = jnp.einsum(
        "bhqk,bqhd->khd", dscores_global, query_blocks, preferred_element_type=jnp.float32
    )
    global_dv = jnp.einsum(
        "bhqk,bqhd->khd", weights_global, grad_blocks, preferred_element_type=jnp.float32
    )
    global_terms = jnp.stack(
        [global_dk.reshape(global_len, width_dev), global_dv.reshape(global_len, width_dev)], 1
    )
    summed_all = lax.psum(global_terms, "seq")
    own_term = lax.dynamic_slice_in_dim(summed_all, my_index * GLEN, GLEN, 0)
    combined = window_sum + random_sum
    base_rows = lax.dynamic_slice_in_dim(combined, own_global * BLK, GLEN, 0)
    combined = lax.dynamic_update_slice_in_dim(combined, base_rows + own_term, own_global * BLK, 0)
    key_grad = combined[:, 0].astype(jnp.bfloat16)
    value_grad = combined[:, 1].astype(jnp.bfloat16)
    return (attn_out, query_grad, key_grad, value_grad)


def solution(mesh):
    in_specs = (
        P("seq", "head"),
        P("seq", "head"),
        P("seq", "head"),
        P("seq", "head"),
        P(),
        P("seq"),
    )
    out_specs = (P("seq", "head"), P("seq", "head"), P("seq", "head"), P("seq", "head"))
    return jax.shard_map(shards, mesh=mesh, in_specs=in_specs, out_specs=out_specs, check_vma=False)
```

profile of v0, /device:TPU:0, one launch (start us, length us, event | category | flops | bytes accessed | tf_op | source)
XLA Modules:
  0.0 270.9 jit_solution(358742052973094636)
XLA Ops:
  7.2 0.8 copy.233
  8.0 1.3 reduce_window_sum.11
  10.4 1.1 pad_maximum_fusion.6
  12.1 1.6 broadcast_select_fusion
  13.8 7.4 %all-to-all-start = ((bf16[8,2,64,2,512]{4,2,3,1,0:T(8,128)(2,1)}), bf16[8,2,64,2,512]{4,2,3,1,0:T(8,128)(2,1)S(1)}, u32[]{:S(2)}, u32[]{:S(2)}) async-start(bf16[8,2,64,2,512]{4,2,3,1,0:T(8,128)(2,1)} %broadcast_select_fusion), calls=%async_computation | async-start | bytes 4194304 | tf_op jit(solution)/shard_map/all_to_all | solution.py:63
  21.9 4.6 %collective-permute-start = (bf16[64,2,512]{2,0,1:T(8,128)(2,1)}, bf16[64,2,512]{2,0,1:T(8,128)(2,1)}, u32[]{:S(2)}, u32[]{:S(2)}) collective-permute-start(bf16[64,2,512]{2,0,1:T(8,128)(2,1)} %get-tuple-element.20), channel_id=1, source_target_pairs={{0,4},{4,8},{8,12},{12,16},{16,20},{20,24},{24,28},{1,5},{5,9},{9,... | collective-permute-start | bytes 393224 | tf_op jit(solution)/shard_map/ppermute | solution.py:20
  26.5 1.3 collective-permute-start.1
  30.2 0.8 copy.257
  31.7 61.0 %all_gather.3 = bf16[128,2,512]{2,1,0:T(2,128)(2,1)S(1)} all-gather(bf16[16,2,512]{2,1,0:T(2,128)(2,1)S(1)} %copy.241), channel_id=1, replica_groups=mesh['seq'=8,'head'=4] {'seq'}, dimensions={0}, use_global_device_ids=true | all-gather | bytes 294912 | tf_op jit(solution)/shard_map/all_gather | solution.py:46
  92.8 1.2 fusion.57
  93.9 1.1 copy.290
  95.0 1.1 copy.291
  96.4 2.0 fusion.59
  98.3 1.2 fusion.58
  99.5 0.8 copy-done.3
  100.6 1.9 pad_maximum_fusion.4
  102.4 1.9 gather_fusion.1
  104.3 1.5 copy.236
  106.1 0.8 copy-done.18
  107.2 1.4 fusion.56
  108.5 0.9 copy.238
  111.8 2.4 fusion.20
  114.3 2.7 copy.237
  116.9 1.2 fusion.54
  118.1 3.7 %fusion.1 = (f32[4,4,64]{2,1,0:T(4,128)}, f32[4,4,384,64]{2,3,1,0:T(8,128)}) fusion(f32[4,4,64]{2,1,0:T(4,128)S(1)} %copy_add_fusion.1, f32[4,4,64]{2,1,0:T(4,128)S(1)} %copy_maximum_fusion, f32[4,4,384,64]{2,3,1,0:T(8,128)S(1)} %get-tuple-element.29, bf16[4,384,4,128]{1,3,2,0:T(8,128)(2,1)} %bitcast.176, bf16[4,64,4,128]{3,2,1,0:T(4,128)(2,1)S(1)} %copy-done.17), kind=kOutput, calls=%fused_computation.15 | convolution fusion | flops 102235136 | bytes 4993024 | tf_op jit(solution)/shard_map/bqhd,bkhd->bhqk/dot_general | solution.py:113
  121.9 2.4 copy.267
  124.3 1.4 multiply_reduce_fusion
  126.4 2.4 fusion.4
  128.8 2.3 fusion.28
  131.1 3.5 %copy.266 = f32[4,384,1,512]{3,1,2,0:T(8,128)} copy(f32[4,384,1,512]{1,3,0,2:T(8,128)} %bitcast.154) | data formatting | bytes 6291456 | tf_op jit(solution)/shard_map/stack;reshape | solution.py:136
  134.7 2.3 fusion
  137.1 1.5 copy-done.6
  138.6 2.8 %copy.272 = bf16[4,192,2,512]{3,2,1,0:T(2,128)(2,1)} copy(bf16[4,192,2,512]{3,1,2,0:T(8,128)(2,1)S(1)} %slice.123) | data formatting | bytes 3145728 | tf_op jit(solution)/shard_map/slice | solution.py:153
  141.5 5.7 %convert_element_type.59 = bf16[12,65536]{1,0:T(8,128)(2,1)} reshape(bf16[4,192,2,512]{3,2,1,0:T(2,128)(2,1)} %copy.272) | data formatting | bytes 3145728 | tf_op jit(solution)/shard_map/convert_element_type | solution.py:153
  147.2 3.8 %convolution_convert_fusion = bf16[16,65536]{1,0:T(8,128)(2,1)} fusion(bf16[12,65536]{1,0:T(8,128)(2,1)} %convert_element_type.59, s32[12]{0:T(128)} %get-tuple-element.24), kind=kOutput, calls=%fused_computation.2 | convolution fusion | flops 26214592 | bytes 3670064 | tf_op jit(solution)/shard_map/ts,tx->sx/dot_general | solution.py:157
  151.0 3.6 %reshape.224 = bf16[8,2,65536]{2,1,0:T(2,128)(2,1)} reshape(bf16[16,65536]{1,0:T(8,128)(2,1)} %convolution_convert_fusion) | data formatting | bytes 4194304 | tf_op jit(solution)/shard_map/reshape | solution.py:161
  154.6 4.4 %all-to-all-start.1 = ((bf16[8,2,65536]{2,1,0:T(2,128)(2,1)}), bf16[8,2,65536]{2,1,0:T(2,128)(2,1)}, u32[]{:S(2)}, u32[]{:S(2)}) async-start(bf16[8,2,65536]{2,1,0:T(2,128)(2,1)} %reshape.224), calls=%async_computation.1 | async-start | bytes 4194304 | tf_op jit(solution)/shard_map/all_to_all | solution.py:160
  159.0 1.3 copy.271
  160.3 1.3 sub.62
  161.6 1.3 copy.260
  162.9 2.0 fusion.48
  164.9 1.8 copy.277
  166.7 1.2 convolution_bitcast_fusion.2
  168.0 2.9 %fusion.11 = bf16[4,64,4,128]{3,1,2,0:T(8,128)(2,1)S(1)} fusion(f32[4,64,4,128]{3,1,2,0:T(8,128)S(1)} %convolution_bitcast_fusion.2, bf16[4,384,4,128]{1,3,2,0:T(8,128)(2,1)} %bitcast.177, f32[4,4,384,64]{2,3,1,0:T(8,128)} %copy-done.2, f32[4,4,64]{2,1,0:T(4,128)S(1)} %copy_add_fusion.1, f32[4,4,64]{2,1,0:T(4,128)S(1)} %copy_maximum_fusion), kind=kOutput, calls=%fused_computation.33 | convolution fusion | flops 102105088 | bytes 3940352 | tf_op jit(solution)/shard_map/bhqk,bkhd->bqhd/dot_general | solution.py:107
  172.1 1.0 fusion.50
  173.0 1.9 copy.276
  174.9 1.9 pad_maximum_fusion.7
  177.0 2.6 fusion.10
  180.7 1.1 copy.268
  181.7 1.0 slice_bitcast_fusion.3
  182.7 3.8 %collective-permute-start.2 = (bf16[64,2,512]{2,0,1:T(8,128)(2,1)S(1)}, bf16[64,2,512]{2,0,1:T(8,128)(2,1)S(1)}, u32[]{:S(2)}, u32[]{:S(2)}) collective-permute-start(bf16[64,2,512]{2,0,1:T(8,128)(2,1)S(1)} %get-tuple-element.10), channel_id=1, source_target_pairs={{0,4},{4,8},{8,12},{12,16},{16,20},{20,24},{24,28},{1,5},{5,9},{9,... | collective-permute-start | bytes 393224 | tf_op jit(solution)/shard_map/ppermute | solution.py:20
  186.5 1.3 collective-permute-start.3
  188.0 0.9 copy.270
  188.9 0.9 copy.269
  189.8 4.0 %collective-permute-done.3 = bf16[64,2,512]{2,0,1:T(8,128)(2,1)S(1)} collective-permute-done((bf16[64,2,512]{2,0,1:T(8,128)(2,1)S(1)}, bf16[64,2,512]{2,0,1:T(8,128)(2,1)S(1)}, u32[]{:S(2)}, u32[]{:S(2)}) %collective-permute-start.3) | collective-permute-done | bytes 131104 | tf_op jit(solution)/shard_map/ppermute | solution.py:21
  193.8 0.8 fusion.33
  194.6 15.2 %all-to-all-done.1 = bf16[8,2,65536]{2,1,0:T(2,128)(2,1)} async-done(((bf16[8,2,65536]{2,1,0:T(2,128)(2,1)}), bf16[8,2,65536]{2,1,0:T(2,128)(2,1)}, u32[]{:S(2)}, u32[]{:S(2)}) %all-to-all-start.1) | async-done | bytes 2097184 | tf_op jit(solution)/shard_map/all_to_all | solution.py:160
  209.8 2.1 reshape.225
  211.8 1.6 fusion.37
  213.4 2.4 reshape.226
  215.8 1.9 fusion.14
  217.7 44.7 %all-reduce.2.cloned.1.call-done = f32[128,2,512]{2,0,1:T(8,128)} async-done(((f32[128,2,512]{2,0,1:T(8,128)}), f32[128,2,512]{2,0,1:T(8,128)}) %all-reduce.2.cloned.1.call-update) | async-done | bytes 524304 | tf_op jit(solution)/shard_map/psum | solution.py:185
  262.4 0.9 add_dynamic-update-slice_fusion
  263.3 0.8 slice_bitcast_fusion
  (111 shorter events, 11.9 us)
Async XLA Ops:
  13.8 7.4 %copy-start.8 = (bf16[256,512]{1,0:T(8,128)(2,1)S(1)}, bf16[256,512]{1,0:T(8,128)(2,1)}, u32[]{:S(2)}) copy-start(bf16[256,512]{1,0:T(8,128)(2,1)} %param.7) | copy-start | bytes 786436
  13.8 7.4 %copy-start.9 = (bf16[256,512]{1,0:T(8,128)(2,1)S(1)}, bf16[256,512]{1,0:T(8,128)(2,1)}, u32[]{:S(2)}) copy-start(bf16[256,512]{1,0:T(8,128)(2,1)} %param.8) | copy-start | bytes 786436
  13.8 88.7 %all-to-all-start = ((bf16[8,2,64,2,512]{4,2,3,1,0:T(8,128)(2,1)}), bf16[8,2,64,2,512]{4,2,3,1,0:T(8,128)(2,1)S(1)}, u32[]{:S(2)}, u32[]{:S(2)}) async-start(bf16[8,2,64,2,512]{4,2,3,1,0:T(8,128)(2,1)} %broadcast_select_fusion), calls=%async_computation | async-start | bytes 4194304 | tf_op jit(solution)/shard_map/all_to_all | solution.py:63
  21.1 8.9 %copy-start.20 = (bf16[256,512]{1,0:T(8,128)(2,1)S(1)}, bf16[256,512]{1,0:T(8,128)(2,1)}, u32[]{:S(2)}) copy-start(bf16[256,512]{1,0:T(8,128)(2,1)} %param.6) | copy-start | bytes 786436
  21.1 9.0 %copy-start.21 = (bf16[256,512]{1,0:T(8,128)(2,1)S(1)}, bf16[256,512]{1,0:T(8,128)(2,1)}, u32[]{:S(2)}) copy-start(bf16[256,512]{1,0:T(8,128)(2,1)} %param.9) | copy-start | bytes 786436
  21.9 78.6 %collective-permute-start = (bf16[64,2,512]{2,0,1:T(8,128)(2,1)}, bf16[64,2,512]{2,0,1:T(8,128)(2,1)}, u32[]{:S(2)}, u32[]{:S(2)}) collective-permute-start(bf16[64,2,512]{2,0,1:T(8,128)(2,1)} %get-tuple-element.20), channel_id=1, source_target_pairs={{0,4},{4,8},{8,12},{12,16},{16,20},{20,24},{24,28},{1,5},{5,9},{9,... | collective-permute-start | bytes 393224 | tf_op jit(solution)/shard_map/ppermute | solution.py:20
  26.5 74.1 %collective-permute-start.1 = (bf16[64,2,512]{2,0,1:T(8,128)(2,1)}, bf16[64,2,512]{2,0,1:T(8,128)(2,1)}, u32[]{:S(2)}, u32[]{:S(2)}) collective-permute-start(bf16[64,2,512]{2,0,1:T(8,128)(2,1)} %get-tuple-element.21), channel_id=1, source_target_pairs={{4,0},{8,4},{12,8},{16,12},{20,16},{24,20},{28,24},{5,1},{9,5},{13... | collective-permute-start | bytes 393224 | tf_op jit(solution)/shard_map/ppermute | solution.py:21
  30.2 65.9 %copy-start.15 = (bf16[4,64,4,128]{3,2,1,0:T(4,128)(2,1)}, bf16[4,64,4,128]{3,2,1,0:T(4,128)(2,1)S(1)}, u32[]{:S(2)}) copy-start(bf16[4,64,4,128]{3,2,1,0:T(4,128)(2,1)S(1)} %reshape.222) | copy-start | bytes 786436
  96.1 4.4 %copy-start.19 = (bf16[128,1,512]{0,2,1:T(8,128)(2,1)}, bf16[128,1,512]{0,2,1:T(8,128)(2,1)S(1)}, u32[]{:S(2)}) copy-start(bf16[128,1,512]{0,2,1:T(8,128)(2,1)S(1)} %copy.291) | copy-start | bytes 393220
  99.5 0.8 copy-start.3
  104.3 1.5 copy-start.24
  105.9 1.0 copy-start.18
  109.4 1.1 copy-start.1
  109.4 1.4 copy-start.4
  110.5 7.6 %copy-start.2 = (f32[4,4,384,64]{2,3,1,0:T(8,128)}, f32[4,4,384,64]{2,3,1,0:T(8,128)S(1)}, u32[]{:S(2)}) copy-start(f32[4,4,384,64]{2,3,1,0:T(8,128)S(1)} %get-tuple-element.29) | copy-start | bytes 4718596
  110.6 1.3 copy-start.16
  114.3 2.7 copy-start.5
  114.3 3.9 %copy-start.17 = (bf16[4,64,4,128]{3,2,1,0:T(4,128)(2,1)S(1)}, bf16[4,64,4,128]{3,2,1,0:T(4,128)(2,1)}, u32[]{:S(2)}) copy-start(bf16[4,64,4,128]{3,2,1,0:T(4,128)(2,1)} %copy-done.15) | copy-start | bytes 786436
  126.4 2.4 copy-start.22
  128.8 2.3 copy-start.7
  136.9 1.7 copy-start.6
  154.6 55.2 %all-to-all-start.1 = ((bf16[8,2,65536]{2,1,0:T(2,128)(2,1)}), bf16[8,2,65536]{2,1,0:T(2,128)(2,1)}, u32[]{:S(2)}, u32[]{:S(2)}) async-start(bf16[8,2,65536]{2,1,0:T(2,128)(2,1)} %reshape.224), calls=%async_computation.1 | async-start | bytes 4194304 | tf_op jit(solution)/shard_map/all_to_all | solution.py:160
  159.0 103.4 %all-reduce.2.cloned.1.call-start = ((), (), s32[]{:S(2)}) async-start(), calls=%async_computation.2 | async-start | bytes 1048576 | tf_op jit(solution)/shard_map/psum | solution.py:185
  168.0 3.9 %copy-start.10 = (f32[4,128,256]{1,2,0:S(1)}, f32[4,128,256]{1,2,0}, u32[]{:S(2)}) copy-start(f32[4,128,256]{1,2,0} %fusion.59) | copy-start | bytes 1572868
  168.0 3.9 %copy-start.11 = (f32[4,4,64,128]{3,2,0,1:T(8,128)S(1)}, f32[4,4,64,128]{3,2,0,1:T(8,128)}, u32[]{:S(2)}) copy-start(f32[4,4,64,128]{3,2,0,1:T(8,128)} %get-tuple-element.5) | copy-start | bytes 1572868
  168.0 3.9 %copy-start.23 = (f32[4,4,64]{2,0,1:T(4,128)S(1)}, f32[4,4,64]{2,0,1:T(4,128)}, u32[]{:S(2)}) copy-start(f32[4,4,64]{2,0,1:T(4,128)} %copy.260) | copy-start | bytes 12292
  172.0 1.0 copy-start.13
  173.0 3.7 %copy-start.14 = (bf16[4,4,64,128]{3,2,0,1:T(8,128)(2,1)S(1)}, bf16[4,4,64,128]{3,2,0,1:T(8,128)(2,1)}, u32[]{:S(2)}) copy-start(bf16[4,4,64,128]{3,2,0,1:T(8,128)(2,1)} %copy-done.13) | copy-start | bytes 786436
  177.0 3.5 %copy-start = (f32[4,384,1,512]{3,1,2,0:T(8,128)S(1)}, f32[4,384,1,512]{3,1,2,0:T(8,128)}, u32[]{:S(2)}) copy-start(f32[4,384,1,512]{3,1,2,0:T(8,128)} %copy.266) | copy-start | bytes 9437188
  182.7 7.1 %collective-permute-start.2 = (bf16[64,2,512]{2,0,1:T(8,128)(2,1)S(1)}, bf16[64,2,512]{2,0,1:T(8,128)(2,1)S(1)}, u32[]{:S(2)}, u32[]{:S(2)}) collective-permute-start(bf16[64,2,512]{2,0,1:T(8,128)(2,1)S(1)} %get-tuple-element.10), channel_id=1, source_target_pairs={{0,4},{4,8},{8,12},{12,16},{16,20},{20,24},{24,28},{1,5},{5,9},{9,... | collective-permute-start | bytes 393224 | tf_op jit(solution)/shard_map/ppermute | solution.py:20
  186.5 7.3 %collective-permute-start.3 = (bf16[64,2,512]{2,0,1:T(8,128)(2,1)S(1)}, bf16[64,2,512]{2,0,1:T(8,128)(2,1)S(1)}, u32[]{:S(2)}, u32[]{:S(2)}) collective-permute-start(bf16[64,2,512]{2,0,1:T(8,128)(2,1)S(1)} %get-tuple-element.11), channel_id=1, source_target_pairs={{4,0},{8,4},{12,8},{16,12},{20,16},{24,20},{28,24},{5,1},{9,5},{13... | collective-permute-start | bytes 393224 | tf_op jit(solution)/shard_map/ppermute | solution.py:21
  194.6 17.3 %copy-start.25 = (s32[16]{0:T(128)S(1)}, s32[16]{0:T(128)}, u32[]{:S(2)}) copy-start(s32[16]{0:T(128)} %sub.62) | copy-start | bytes 196
  213.4 2.4 copy-start.12
Sparse Core Ops, SparseCore 0:
  176.9 85.3 all-reduce.1
where the time goes:
time: 272 us; the launch traced here: 271 us
  waiting for transfers between devices  63.9 us (23%)
  blocking collectives  61 us (22%)
  local copies, waits for them, and re-layouts  57.8 us (21%)
  matrix products  27.4 us (10%)
  other arithmetic  23 us (8%)
  starting transfers between devices  22.7 us (8%)
  between operations  15.2 us (6%)
    all_gather x1, blocking collectives, shards(): global_kv = lax.all_gather(mine, 'seq', axis=0, tiled=True)  61 us
    psum x1, waiting for transfers between devices, shards(): summed_all = lax.psum(global_terms, 'seq')  44.7 us
    all_to_all x1, waiting for transfers between devices, shards(): lax.all_to_all(to_send.reshape(seq_count, capacity, BLK * 2 * width_dev),...  15.2 us
    unnamed x57, local copies, waits for them, and re-layouts  8.55 us
    ppermute x2, starting transfers between devices, extended(): before = lax.ppermute(last, axis, up)  8.31 us
    all_to_all x1, starting transfers between devices, shards(): lax.all_to_all(outgoing, 'seq', split_axis=0, concat_axis=0, tiled=True)  7.38 us
    another operation x2, local copies, waits for them, and re-layouts, shards(): jnp.stack([local_dk.reshape(blocks_dev, local_len, width_dev), local_dv.r...  5.89 us
    convert_element_type x1, local copies, waits for them, and re-layouts, shards(): local_grads[:, 3 * BLK:].reshape(spots, BLK * 2 * width_dev)  5.73 us
  transfers between devices with their start and end apart: 7, of which 3 were waited for; matrix products, arithmetic and copies ran while one was open for 17% of the time, Pallas kernels for 0%

commit v1 on v0

v1 whole, which is shorter than its diff:
```python
import functools
import math

import jax
import jax.numpy as jnp
from jax import lax
from jax.experimental import pallas as pl
from jax.experimental.pallas import tpu as pltpu
from jax.sharding import PartitionSpec as P

HDIM = 128
BLK = 64
GLEN = 16
MESH = pl.DeviceIdType.MESH
F32 = jnp.float32
BF16 = jnp.bfloat16


def dot(a, b, dims):
    return lax.dot_general(a, b, (dims, ((), ())), preferred_element_type=F32)


def kernel(
    nz, nx, nb, per, cap, heads,
    rb_ref, gb_ref, q_ref, k_ref, v_ref, g_ref,
    o_ref, dq_ref, dk_ref, dv_ref,
    col, xs, xr, yr, hr, wh, wr, rin, rout, wacc, gath, gkv, tmp, tr, gacc,
    tgt, inv, place,
    z_send, z_recv, x_send, x_recv, y_send, y_recv, h_send, h_recv, w_send, w_recv, r_send, r_recv,
):
    n = nz * nx
    rows = nb * BLK
    spots = nb * per
    ext = rows + GLEN
    scale = 1.0 / math.sqrt(HDIM)
    me = lax.axis_index("seq")
    z = me // nx
    x = me % nx

    def lanes(h):
        return pl.ds(pl.multiple_of(h * HDIM, HDIM), HDIM)

    def remote(src, dst, send, recv, dev):
        return pltpu.make_async_remote_copy(
            src_ref=src, dst_ref=dst, send_sem=send, recv_sem=recv,
            device_id={"seq": dev}, device_id_type=MESH,
        )

    barrier = pltpu.get_barrier_semaphore()
    for step in range(1, n):
        pl.semaphore_signal(
            barrier, inc=1, device_id={"seq": lax.rem(me + step, n)}, device_id_type=MESH
        )
    own_global = gb_ref[0] - me * nb

    def pack_own(h, _):
        for kv, ref in enumerate((k_ref, v_ref)):
            col[h, z, kv, 0:rows, :] = ref[:, lanes(h)]
            picked = ref[0:GLEN, lanes(h)]
            for blk in range(1, nb):
                at = slice(blk * BLK, blk * BLK + GLEN)
                picked = jnp.where(own_global == blk, ref[at, lanes(h)], picked)
            col[h, z, kv, rows:ext, :] = picked
        return 0

    lax.fori_loop(0, heads, pack_own, 0)
    pl.semaphore_wait(barrier, n - 1)

    def z_copy(h, zz, up):
        dev = me + (nx if up else -nx)
        return remote(
            col.at[h, zz], col.at[h, zz], z_send.at[h, zz, int(up)], z_recv.at[h, zz], dev
        )

    def halo_copy(h, nxt):
        edge = pl.ds(rows - BLK, BLK) if nxt else pl.ds(0, BLK)
        slot = 0 if nxt else 1
        return remote(
            col.at[h, z, :, edge, :], hr.at[h, slot],
            h_send.at[h, slot], h_recv.at[h, slot], me + (1 if nxt else -1),
        )

    def first_sends(h, _):
        @pl.when(z < nz - 1)
        def _():
            z_copy(h, z, True).start()

        @pl.when(z > 0)
        def _():
            z_copy(h, z, False).start()

        @pl.when(me < n - 1)
        def _():
            halo_copy(h, True).start()

        @pl.when(me > 0)
        def _():
            halo_copy(h, False).start()

        return 0

    lax.fori_loop(0, heads, first_sends, 0)

    @pl.when(me == 0)
    def _():
        hr[:, 0] = jnp.zeros_like(hr[:, 0])

    @pl.when(me == n - 1)
    def _():
        hr[:, 1] = jnp.zeros_like(hr[:, 1])

    def own_entry(t):
        return rb_ref[me * nb + t // per, t % per]

    for t in range(spots):
        owner = lax.div(own_entry(t), nb)
        rank = jnp.int32(0)
        for s in range(t):
            rank = rank + (lax.div(own_entry(s), nb) == owner).astype(jnp.int32)
        place[t] = owner * cap + rank

    def fill_inv(j, _):
        count = jnp.int32(0)
        found = [jnp.int32(spots)] * cap
        for t in range(spots):
            hit = lax.div(own_entry(t), nb) == j
            for c in range(cap):
                found[c] = jnp.where(hit & (count == c), jnp.int32(t), found[c])
            count = count + hit.astype(jnp.int32)
        for c in range(cap):
            inv[j * cap + c] = found[c]
        return 0

    lax.fori_loop(0, n, fill_inv, 0)

    def fill_tgt(at, _):
        px = at // nz
        zz = at % nz
        j = zz * nx + x
        count = jnp.int32(0)
        found = [jnp.int32(-1)] * cap
        for t in range(spots):
            block = rb_ref[(z * nx + px) * nb + t // per, t % per]
            hit = lax.div(block, nb) == j
            for c in range(cap):
                found[c] = jnp.where(hit & (count == c), block - j * nb, found[c])
            count = count + hit.astype(jnp.int32)
        for c in range(cap):
            tgt[at * cap + c] = found[c]
        return 0

    lax.fori_loop(0, nx * nz, fill_tgt, 0)
    tr[spots] = jnp.zeros_like(tr[spots])

    def x_copy(h, px, zz):
        return remote(
            xs.at[h, px, zz], xr.at[h, x, zz], x_send.at[h, px, zz], x_recv.at[h, x, zz],
            z * nx + px,
        )

    def x_wait(h, xo, zz):
        remote(
            xs.at[h, xo, zz], xr.at[h, xo, zz], x_send.at[h, xo, zz], x_recv.at[h, xo, zz],
            z * nx + xo,
        ).wait_recv()

    def y_copy(h, xo, zz):
        return remote(
            xs.at[h, xo, zz], yr.at[h, x, zz], y_send.at[h, xo, zz], y_recv.at[h, x, zz],
            z * nx + xo,
        )

    def y_wait(h, d, zz):
        remote(
            xs.at[h, d, zz], yr.at[h, d, zz], y_send.at[h, d, zz], y_recv.at[h, d, zz],
            z * nx + d,
        ).wait_recv()

    def serve(h, zz):
        for blk in range(nb):
            tmp[blk] = col[h, zz, :, blk * BLK : (blk + 1) * BLK, :]

        def one(px, _):
            def put(dst):
                for c in range(cap):
                    block = jnp.maximum(tgt[(px * nz + zz) * cap + c], 0)
                    dst[h, px, zz, :, c * BLK : (c + 1) * BLK, :] = tmp[block]
                dst[h, px, zz, :, cap * BLK :, :] = col[h, zz, :, rows:ext, :]

            @pl.when(px == x)
            def _():
                put(xr)

            @pl.when(px != x)
            def _():
                put(xs)
                x_copy(h, px, zz).start()

            return 0

        lax.fori_loop(0, nx, one, 0)

    def gather_stage(h):
        serve(h, z)

        def one(s, _):
            @pl.when(z - s >= 0)
            def _():
                zz = z - s
                z_copy(h, zz, True).wait_recv()

                @pl.when(z < nz - 1)
                def _():
                    z_copy(h, zz, True).start()

                serve(h, zz)

            @pl.when(z + s < nz)
            def _():
                zz = z + s
                z_copy(h, zz, False).wait_recv()

                @pl.when(z > 0)
                def _():
                    z_copy(h, zz, False).start()

                serve(h, zz)

            return 0

        lax.fori_loop(1, nz, one, 0)

    def w_copy(h, nxt):
        slot = 1 if nxt else 0
        return remote(
            wh.at[h, slot], wr.at[h, slot], w_send.at[h, slot], w_recv.at[h, slot],
            me + (1 if nxt else -1),
        )

    def compute_stage(h):
        def collect(j, _):
            zz = j // nx
            xo = j % nx

            @pl.when(xo != x)
            def _():
                x_wait(h, xo, zz)

            for c in range(cap):
                gath[j * cap + c] = xr[h, xo, zz, :, c * BLK : (c + 1) * BLK, :]
            gkv[:, pl.ds(pl.multiple_of(j * GLEN, GLEN), GLEN), :] = xr[h, xo, zz, :, cap * BLK :, :]
            return 0

        lax.fori_loop(0, n, collect, 0)

        @pl.when(me > 0)
        def _():
            halo_copy(h, True).wait_recv()

        @pl.when(me < n - 1)
        def _():
            halo_copy(h, False).wait_recv()

        def window(blk):
            if blk < 0:
                return hr[h, 0]
            if blk >= nb:
                return hr[h, 1]
            return col[h, z, :, blk * BLK : (blk + 1) * BLK, :]

        wacc[h] = jnp.zeros_like(wacc[h])
        length = (3 + per) * BLK + n * GLEN
        column = lax.broadcasted_iota(jnp.int32, (BLK, length), 1)
        low = (3 + per) * BLK
        gsum_k = gsum_v = None
        for b in range(nb):
            parts = [window(b - 1), window(b), window(b + 1)]
            parts += [gath[place[b * per + r]] for r in range(per)]
            parts.append(gkv[...])
            kcat = jnp.concatenate([p[0] for p in parts], 0)
            vcat = jnp.concatenate([p[1] for p in parts], 0)
            at = slice(b * BLK, (b + 1) * BLK)
            q = q_ref[at, lanes(h)]
            g = g_ref[at, lanes(h)]
            s = dot(q, kcat, ((1,), (1,))) * scale
            if b == 0:
                s = jnp.where((column < BLK) & (me == 0), -jnp.inf, s)
            if b == nb - 1:
                s = jnp.where(
                    (column >= 2 * BLK) & (column < 3 * BLK) & (me == n - 1), -jnp.inf, s
                )
            e = jnp.exp(s - jnp.max(s, axis=1, keepdims=True))
            p = e * (1.0 / jnp.sum(e, axis=1, keepdims=True))
            pb = p.astype(BF16)
            o_ref[at, lanes(h)] = dot(pb, vcat, ((1,), (0,))).astype(BF16)
            dp = dot(g, vcat, ((1,), (1,)))
            delta = jnp.sum(p * dp, axis=1, keepdims=True)
            ds = (p * (dp - delta) * scale).astype(BF16)
            dq_ref[at, lanes(h)] = dot(ds, kcat, ((1,), (0,))).astype(BF16)
            dk = dot(ds, q, ((0,), (0,)))
            dv = dot(pb, g, ((0,), (0,)))
            for kv, term in ((0, dk), (1, dv)):
                wacc[h, kv, b * BLK : (b + 3) * BLK, :] += term[: 3 * BLK]
                for r in range(per):
                    tr[b * per + r, kv] = term[(3 + r) * BLK : (4 + r) * BLK].astype(BF16)
            gsum_k = dk[low:] if b == 0 else gsum_k + dk[low:]
            gsum_v = dv[low:] if b == 0 else gsum_v + dv[low:]
        gacc[0] = gsum_k.astype(BF16)
        gacc[1] = gsum_v.astype(BF16)

        def give(j, _):
            zz = j // nx
            xo = j % nx

            def put(dst):
                for c in range(cap):
                    dst[h, xo, zz, :, c * BLK : (c + 1) * BLK, :] = tr[inv[j * cap + c]]
                dst[h, xo, zz, :, cap * BLK :, :] = gacc[
                    :, pl.ds(pl.multiple_of(j * GLEN, GLEN), GLEN), :
                ]

            @pl.when(xo == x)
            def _():
                put(yr)

            @pl.when(xo != x)
            def _():
                x_copy(h, xo, zz).wait_send()
                put(xs)
                y_copy(h, xo, zz).start()

            return 0

        lax.fori_loop(0, n, give, 0)

        @pl.when(me > 0)
        def _():
            wh[h, 0] = wacc[h, :, 0:BLK, :].astype(BF16)
            w_copy(h, False).start()

        @pl.when(me < n - 1)
        def _():
            wh[h, 1] = wacc[h, :, rows + BLK :, :].astype(BF16)
            w_copy(h, True).start()

    def column_terms(h, zz):
        pieces = []
        slots = [
            (tgt[(d * nz + zz) * cap + c], yr[h, d, zz, :, c * BLK : (c + 1) * BLK, :].astype(F32))
            for d in range(nx)
            for c in range(cap)
        ]
        for blk in range(nb):
            total = None
            for target, term in slots:
                part = jnp.where(target == blk, term, 0.0)
                total = part if total is None else total + part
            pieces.append(total)
        total = None
        for d in range(nx):
            part = yr[h, d, zz, :, cap * BLK :, :].astype(F32)
            total = part if total is None else total + part
        return pieces, total

    def r_copy(h, zz, slot, up):
        return remote(
            rout.at[h, zz], rin.at[h, slot], r_send.at[h, zz], r_recv.at[h, slot],
            me + (nx if up else -nx),
        )

    def pass_on(h, zz, more):
        pieces, glob = column_terms(h, zz)

        def put(extra):
            for blk in range(nb):
                at = slice(blk * BLK, (blk + 1) * BLK)
                rout[h, zz, :, at, :] = extra(pieces[blk], at).astype(BF16)
            rout[h, zz, :, rows:ext, :] = extra(glob, slice(rows, ext)).astype(BF16)

        @pl.when(more)
        def _():
            r_copy(h, zz, zz, False).wait_recv()
            put(lambda v, at: v + rin[h, zz, :, at, :].astype(F32))

        @pl.when(jnp.logical_not(more))
        def _():
            put(lambda v, at: v)

    def return_stage(h):
        def arrive(at, _):
            d = at // nz

            @pl.when(d != x)
            def _():
                y_wait(h, d, at % nz)

            return 0

        lax.fori_loop(0, nx * nz, arrive, 0)

        def one(i, _):
            down = i
            up = nz - 1 - i

            @pl.when(down < z)
            def _():
                pass_on(h, down, z < nz - 1)
                r_copy(h, down, down, False).start()

            @pl.when(up > z)
            def _():
                pass_on(h, up, z > 0)

                @pl.when(up == z + 1)
                def _():
                    r_copy(h, up, nz, True).start()

                @pl.when(up != z + 1)
                def _():
                    r_copy(h, up, up, True).start()

            return 0

        lax.fori_loop(0, nz - 1, one, 0)

        pieces, glob = column_terms(h, z)
        for blk in range(nb):
            at = slice(blk * BLK, (blk + 1) * BLK)
            wacc[h, :, BLK + blk * BLK : 2 * BLK + blk * BLK, :] += pieces[blk]

        @pl.when(me > 0)
        def _():
            w_copy(h, True).wait_recv()
            wacc[h, :, BLK : 2 * BLK, :] += wr[h, 1].astype(F32)

        @pl.when(me < n - 1)
        def _():
            w_copy(h, False).wait_recv()
            wacc[h, :, rows : rows + BLK, :] += wr[h, 0].astype(F32)

        @pl.when(z == nz - 1)
        def _():
            rin[h, z] = jnp.zeros_like(rin[h, z])

        @pl.when(z < nz - 1)
        def _():
            r_copy(h, z, z, False).wait_recv()

        @pl.when(z == 0)
        def _():
            rin[h, nz] = jnp.zeros_like(rin[h, nz])

        @pl.when(z > 0)
        def _():
            r_copy(h, z, nz, True).wait_recv()

        glob = glob + rin[h, z, :, rows:ext, :].astype(F32) + rin[h, nz, :, rows:ext, :].astype(F32)
        for blk in range(nb):
            at = slice(blk * BLK, (blk + 1) * BLK)
            total = (
                wacc[h, :, BLK + blk * BLK : 2 * BLK + blk * BLK, :]
                + rin[h, z, :, at, :].astype(F32)
                + rin[h, nz, :, at, :].astype(F32)
            )
            top = total[:, :GLEN] + jnp.where(own_global == blk, glob, 0.0)
            total = jnp.concatenate([top, total[:, GLEN:]], 1).astype(BF16)
            dk_ref[at, lanes(h)] = total[0]
            dv_ref[at, lanes(h)] = total[1]

    def turn(t, _):
        @pl.when(t < heads)
        def _():
            gather_stage(t)

        @pl.when((t >= 1) & (t <= heads))
        def _():
            compute_stage(t - 1)

        @pl.when(t >= 2)
        def _():
            return_stage(t - 2)

        return 0

    lax.fori_loop(0, heads + 2, turn, 0)

    def drain(h, _):
        def shard(zz, _):
            @pl.when((zz <= z) & (z < nz - 1))
            def _():
                z_copy(h, zz, True).wait_send()

            @pl.when((zz >= z) & (z > 0))
            def _():
                z_copy(h, zz, False).wait_send()

            @pl.when(zz != z)
            def _():
                r_copy(h, zz, zz, False).wait_send()

            def partner(px, _):
                @pl.when(px != x)
                def _():
                    y_copy(h, px, zz).wait_send()

                return 0

            lax.fori_loop(0, nx, partner, 0)
            return 0

        lax.fori_loop(0, nz, shard, 0)

        @pl.when(me < n - 1)
        def _():
            halo_copy(h, True).wait_send()
            w_copy(h, True).wait_send()

        @pl.when(me > 0)
        def _():
            halo_copy(h, False).wait_send()
            w_copy(h, False).wait_send()

        return 0

    lax.fori_loop(0, heads, drain, 0)


def grid_of(n):
    nx = 1
    while nx * nx * 4 <= n and n % (nx * 2) == 0:
        nx *= 2
    return n // nx, nx


def shards(n, queries, keys, values, out_grad, rand_blocks, glob_blocks):
    rows, width = queries.shape
    heads = width // HDIM
    nb = rows // BLK
    per = rand_blocks.shape[1]
    spots = nb * per
    cap = max(2, (spots + n - 1) // n)
    nz, nx = grid_of(n)
    ext = rows + GLEN
    xrows = cap * BLK + GLEN
    out = jax.ShapeDtypeStruct((rows, width), BF16)
    vmem = pl.BlockSpec(memory_space=pltpu.VMEM)
    smem = pl.BlockSpec(memory_space=pltpu.SMEM)
    dma = pltpu.SemaphoreType.DMA
    slots = pltpu.VMEM((heads, nx, nz, 2, xrows, HDIM), BF16)
    edges = pltpu.VMEM((heads, 2, 2, BLK, HDIM), BF16)
    return pl.pallas_call(
        functools.partial(kernel, nz, nx, nb, per, cap, heads),
        out_shape=[out] * 4,
        in_specs=[smem, smem, vmem, vmem, vmem, vmem],
        out_specs=[vmem] * 4,
        scratch_shapes=[
            pltpu.VMEM((heads, nz, 2, ext, HDIM), BF16),
            slots, slots, slots,
            edges, edges, edges,
            pltpu.VMEM((heads, nz + 1, 2, ext, HDIM), BF16),
            pltpu.VMEM((heads, nz, 2, ext, HDIM), BF16),
            pltpu.VMEM((heads, 2, rows + 2 * BLK, HDIM), F32),
            pltpu.VMEM((n * cap, 2, BLK, HDIM), BF16),
            pltpu.VMEM((2, n * GLEN, HDIM), BF16),
            pltpu.VMEM((nb, 2, BLK, HDIM), BF16),
            pltpu.VMEM((spots + 1, 2, BLK, HDIM), BF16),
            pltpu.VMEM((2, n * GLEN, HDIM), BF16),
            pltpu.SMEM((nx * nz * cap,), jnp.int32),
            pltpu.SMEM((n * cap,), jnp.int32),
            pltpu.SMEM((spots,), jnp.int32),
            dma((heads, nz, 2)), dma((heads, nz)),
            dma((heads, nx, nz)), dma((heads, nx, nz)),
            dma((heads, nx, nz)), dma((heads, nx, nz)),
            dma((heads, 2)), dma((heads, 2)),
            dma((heads, 2)), dma((heads, 2)),
            dma((heads, nz)), dma((heads, nz + 1)),
        ],
        compiler_params=pltpu.CompilerParams(
            collective_id=0, has_side_effects=True, vmem_limit_bytes=60 * 1024 * 1024
        ),
    )(rand_blocks, glob_blocks, queries, keys, values, out_grad)


def solution(mesh):
    split = P("seq", "head")
    return jax.shard_map(
        functools.partial(shards, mesh.shape["seq"]),
        mesh=mesh,
        in_specs=(split, split, split, split, P(), P("seq")),
        out_specs=(split, split, split, split),
        check_vma=False,
    )
```

time: 272 us -> 145 us (0.53)
  Pallas kernels: 0 us -> 135 us
  waiting for transfers between devices: 63.9 us -> 0 us
  blocking collectives: 61 us -> 0 us
  local copies, waits for them, and re-layouts: 57.8 us -> 5.87 us
  matrix products: 27.4 us -> 0 us
  other arithmetic: 23 us -> 0 us
  starting transfers between devices: 22.7 us -> 0 us
  between operations: 15.2 us -> 1.3 us
    pallas_call x0 -> x1, Pallas kernels: none -> 135 us  [shards(): pl.pallas_call(functools.partial(kernel, nz, nx, nb, per, cap, heads), ou...]
    all_gather x1 -> x0, blocking collectives: 61 us -> none  [shards(): global_kv = lax.all_gather(mine, 'seq', axis=0, tiled=True)]
    psum x1 -> x0, waiting for transfers between devices: 44.7 us -> none  [shards(): summed_all = lax.psum(global_terms, 'seq')]
    dot_general x12 -> x0, matrix products: 24.3 us -> none  [the longest x1 3.81 us: shards(): jnp.einsum('ts,tx->sx', placing, slot_grads, preferred_element_type=jnp.f...]
    all_to_all x2 -> x0, waiting for transfers between devices: 15.2 us -> none  [the longest x1 15.2 us: shards(): lax.all_to_all(to_send.reshape(seq_count, capacity, BLK * 2 * width_dev),...]
    slice x10 -> x0, local copies, waits for them, and re-layouts: 12.9 us -> none  [the longest x2 4.02 us: shards(): local_kv[:, :, 1].reshape(blocks_dev, local_len, head_count, HDIM)]
    all_to_all x2 -> x0, starting transfers between devices: 11.7 us -> none  [the longest x1 7.38 us: shards(): lax.all_to_all(outgoing, 'seq', split_axis=0, concat_axis=0, tiled=True)]
    ppermute x4 -> x0, starting transfers between devices: 10.9 us -> none  [the longest x2 8.31 us: extended(): before = lax.ppermute(last, axis, up)]
  transfers between devices with their start and end apart: 7 -> 0, of which waited for: 3 -> 0; matrix products, arithmetic and copies ran while one was open for 17% -> 0% of each run, Pallas kernels for 0% -> 0%
where the time goes in v1:
time: 145 us; the launch traced here: 143 us
  Pallas kernels  135 us (93%)
  local copies, waits for them, and re-layouts  5.87 us (4%)
    pallas_call x1, Pallas kernels, shards(): pl.pallas_call(functools.partial(kernel, nz, nx, nb, per, cap, heads), ou...  135 us
    unnamed x11, local copies, waits for them, and re-layouts  5.87 us

profile of v1, /device:TPU:0, one launch (start us, length us, event | category | flops | bytes accessed | tf_op | source)
XLA Modules:
  0.0 142.6 jit_solution(16138435981951601002)
XLA Ops:
  1.3 1.4 copy.10.rb_ref
  2.6 135.4 %shard_map.93 = (bf16[256,512]{1,0:T(8,128)(2,1)}, bf16[256,512]{1,0:T(8,128)(2,1)}, bf16[256,512]{1,0:T(8,128)(2,1)}, bf16[256,512]{1,0:T(8,128)(2,1)}) custom-call(s32[32,3]{1,0:T(8,128)} %copy.10.rb_ref, s32[1]{0:T(128)S(6)} %copy.15.gb_ref, bf16[256,512]{1,0:T(8,128)(2,1)} %q_ref.1, bf16[256,512]{1,0:T(8,128)(2,1)} %k_ref.1, bf16[256,512]{1,0:T(8,128)(2,1)} %v_ref.1, ...), custom_call_target="tpu_custom_call" | custom-call | tf_op jit(solution)/shard_map/pallas_call | solution.py:551
  138.0 0.0 copy-start.2
  138.1 1.7 %copy.16 = bf16[256,512]{1,0:T(8,128)(2,1)} copy(bf16[256,512]{1,0:T(8,128)(2,1)} %get-tuple-element.8) | data formatting | bytes 524288
  139.8 0.0 copy-done.2
  139.8 0.0 copy-start.1
  139.8 0.7 copy.17
  140.5 0.3 copy-done.1
  140.8 0.0 copy-start
  140.8 0.7 copy.18
  141.5 0.3 copy-done
  141.9 0.7 copy.19
Async XLA Ops:
  138.0 1.7 %copy-start.2 = (bf16[256,512]{1,0:T(8,128)(2,1)S(1)}, bf16[256,512]{1,0:T(8,128)(2,1)}, u32[]{:S(2)}) copy-start(bf16[256,512]{1,0:T(8,128)(2,1)} %get-tuple-element.9) | copy-start | bytes 786436
  139.8 1.0 copy-start.1
  140.8 1.0 copy-start

commit v2 on v1

--- a/solution.py
+++ b/solution.py
@@ -33,6 +33,7 @@
     spots = nb * per
     ext = rows + GLEN
     scale = 1.0 / math.sqrt(HDIM)
+    lead = 2
     me = lax.axis_index("seq")
     z = me // nx
     x = me % nx
@@ -99,7 +100,7 @@
 
         return 0
 
-    lax.fori_loop(0, heads, first_sends, 0)
+    lax.fori_loop(0, min(lead, heads), first_sends, 0)
 
     @pl.when(me == 0)
     def _():
@@ -200,11 +201,19 @@
 
         lax.fori_loop(0, nx, one, 0)
 
-    def gather_stage(h):
-        serve(h, z)
-
+    def gather_stage(t):
         def one(s, _):
-            @pl.when(z - s >= 0)
+            h = t + nz - 1 - s
+
+            @pl.when((h >= 0) & (h < heads) & (s == 1))
+            def _():
+                @pl.when(h + lead < heads)
+                def _():
+                    first_sends(h + lead, 0)
+
+                serve(h, z)
+
+            @pl.when((h >= 0) & (h < heads) & (z - s >= 0))
             def _():
                 zz = z - s
                 z_copy(h, zz, True).wait_recv()
@@ -215,7 +224,7 @@
 
                 serve(h, zz)
 
-            @pl.when(z + s < nz)
+            @pl.when((h >= 0) & (h < heads) & (z + s < nz))
             def _():
                 zz = z + s
                 z_copy(h, zz, False).wait_recv()
@@ -386,28 +395,17 @@
         def _():
             put(lambda v, at: v)
 
-    def return_stage(h):
-        def arrive(at, _):
-            d = at // nz
-
-            @pl.when(d != x)
-            def _():
-                y_wait(h, d, at % nz)
-
-            return 0
-
-        lax.fori_loop(0, nx * nz, arrive, 0)
-
-        def one(i, _):
-            down = i
-            up = nz - 1 - i
-
-            @pl.when(down < z)
+    def pass_stage(h):
+        def one(u, _):
+            down = u - (nz - 1 - z)
+            up = nz - 1 - (u - z)
+
+            @pl.when((down >= 0) & (down < z))
             def _():
                 pass_on(h, down, z < nz - 1)
                 r_copy(h, down, down, False).start()
 
-            @pl.when(up > z)
+            @pl.when((up > z) & (up < nz))
             def _():
                 pass_on(h, up, z > 0)
 
@@ -421,8 +419,21 @@
 
             return 0
 
-        lax.fori_loop(0, nz - 1, one, 0)
-
+        lax.fori_loop(0, 2 * nz - 2, one, 0)
+
+    def arrive_stage(h):
+        def arrive(at, _):
+            d = at // nz
+
+            @pl.when(d != x)
+            def _():
+                y_wait(h, d, at % nz)
+
+            return 0
+
+        lax.fori_loop(0, nx * nz, arrive, 0)
+
+    def final_stage(h):
         pieces, glob = column_terms(h, z)
         for blk in range(nb):
             at = slice(blk * BLK, (blk + 1) * BLK)
@@ -467,22 +478,41 @@
             dk_ref[at, lanes(h)] = total[0]
             dv_ref[at, lanes(h)] = total[1]
 
-    def turn(t, _):
-        @pl.when(t < heads)
-        def _():
-            gather_stage(t)
-
-        @pl.when((t >= 1) & (t <= heads))
-        def _():
-            compute_stage(t - 1)
-
-        @pl.when(t >= 2)
-        def _():
-            return_stage(t - 2)
+    outer = (z == 0) | (z == nz - 1)
+
+    def sums(h, mine):
+        @pl.when((h >= 0) & (h < heads) & mine)
+        def _():
+            arrive_stage(h)
+            pass_stage(h)
+
+    def turn(i, _):
+        t = i - (nz - 2)
+
+        def half(part, _):
+            @pl.when((part == 0) == outer)
+            def _():
+                sums(t - 2, True)
+
+            @pl.when(part == 0)
+            def _():
+                gather_stage(t)
+
+                @pl.when((t >= 1) & (t <= heads))
+                def _():
+                    compute_stage(t - 1)
+
+            return 0
+
+        lax.fori_loop(0, 2, half, 0)
+
+        @pl.when(t >= 3)
+        def _():
+            final_stage(t - 3)
 
         return 0
 
-    lax.fori_loop(0, heads + 2, turn, 0)
+    lax.fori_loop(0, heads + 3 + nz - 2, turn, 0)
 
     def drain(h, _):
         def shard(zz, _):

time: 145 us -> 104 us (0.72); the launches traced: 143 us -> 104 us
  Pallas kernels: 135 us -> 96.6 us
    pallas_call x1, Pallas kernels: 135 us -> 96.6 us  [shards(): pl.pallas_call(functools.partial(kernel, nz, nx, nb, per, cap, heads), ou...]
where the time goes in v2:
time: 104 us
  Pallas kernels  96.6 us (93%)
  local copies, waits for them, and re-layouts  5.87 us (6%)
  between operations  1.3 us (1%)
    pallas_call x1, Pallas kernels, shards(): pl.pallas_call(functools.partial(kernel, nz, nx, nb, per, cap, heads), ou...  96.6 us
    unnamed x11, local copies, waits for them, and re-layouts  5.87 us

profile of v2, /device:TPU:0, one launch (start us, length us, event | category | flops | bytes accessed | tf_op | source)
XLA Modules:
  0.0 103.8 jit_solution(6365440103646015619)
XLA Ops:
  1.3 1.4 %copy.10.rb_ref = s32[32,3]{1,0:T(8,128)} copy(s32[32,3]{0,1:T(4,128)} %param.10) | data formatting | bytes 768 | tf_op args[4]
  2.6 96.6 %shard_map.93 = (bf16[256,512]{1,0:T(8,128)(2,1)}, bf16[256,512]{1,0:T(8,128)(2,1)}, bf16[256,512]{1,0:T(8,128)(2,1)}, bf16[256,512]{1,0:T(8,128)(2,1)}) custom-call(s32[32,3]{1,0:T(8,128)} %copy.10.rb_ref, s32[1]{0:T(128)S(6)} %copy.15.gb_ref, bf16[256,512]{1,0:T(8,128)(2,1)} %q_ref.1, bf16[256,512]{1,0:T(8,128)(2,1)} %k_ref.1, bf16[256,512]{1,0:T(8,128)(2,1)} %v_ref.1, ...), custom_call_target="tpu_custom_call" | custom-call | tf_op jit(solution)/shard_map/pallas_call | solution.py:581
  99.3 0.0 copy-start.2
  99.3 1.7 %copy.16 = bf16[256,512]{1,0:T(8,128)(2,1)} copy(bf16[256,512]{1,0:T(8,128)(2,1)} %get-tuple-element.8) | data formatting | bytes 524288
  101.0 0.0 copy-done.2
  101.0 0.0 copy-start.1
  101.0 0.7 copy.17
  101.7 0.3 copy-done.1
  102.1 0.0 copy-start
  102.1 0.7 copy.18
  102.8 0.3 copy-done
  103.1 0.7 copy.19
Async XLA Ops:
  99.3 1.7 %copy-start.2 = (bf16[256,512]{1,0:T(8,128)(2,1)S(1)}, bf16[256,512]{1,0:T(8,128)(2,1)}, u32[]{:S(2)}) copy-start(bf16[256,512]{1,0:T(8,128)(2,1)} %get-tuple-element.9) | copy-start | bytes 786436
  101.0 1.0 %copy-start.1 = (bf16[256,512]{1,0:T(8,128)(2,1)S(1)}, bf16[256,512]{1,0:T(8,128)(2,1)}, u32[]{:S(2)}) copy-start(bf16[256,512]{1,0:T(8,128)(2,1)} %get-tuple-element.10) | copy-start | bytes 786436
  102.1 1.0 %copy-start = (bf16[256,512]{1,0:T(8,128)(2,1)S(1)}, bf16[256,512]{1,0:T(8,128)(2,1)}, u32[]{:S(2)}) copy-start(bf16[256,512]{1,0:T(8,128)(2,1)} %get-tuple-element.11) | copy-start | bytes 786436

commit v3 on v2

--- a/solution.py
+++ b/solution.py
@@ -353,6 +353,14 @@
             w_copy(h, True).start()
 
     def column_terms(h, zz):
+        def arrive(d, _):
+            @pl.when(d != x)
+            def _():
+                y_wait(h, d, zz)
+
+            return 0
+
+        lax.fori_loop(0, nx, arrive, 0)
         pieces = []
         slots = [
             (tgt[(d * nz + zz) * cap + c], yr[h, d, zz, :, c * BLK : (c + 1) * BLK, :].astype(F32))
@@ -421,18 +429,6 @@
 
         lax.fori_loop(0, 2 * nz - 2, one, 0)
 
-    def arrive_stage(h):
-        def arrive(at, _):
-            d = at // nz
-
-            @pl.when(d != x)
-            def _():
-                y_wait(h, d, at % nz)
-
-            return 0
-
-        lax.fori_loop(0, nx * nz, arrive, 0)
-
     def final_stage(h):
         pieces, glob = column_terms(h, z)
         for blk in range(nb):
@@ -483,28 +479,18 @@
     def sums(h, mine):
         @pl.when((h >= 0) & (h < heads) & mine)
         def _():
-            arrive_stage(h)
             pass_stage(h)
 
     def turn(i, _):
         t = i - (nz - 2)
 
-        def half(part, _):
-            @pl.when((part == 0) == outer)
-            def _():
-                sums(t - 2, True)
-
-            @pl.when(part == 0)
-            def _():
-                gather_stage(t)
-
-                @pl.when((t >= 1) & (t <= heads))
-                def _():
-                    compute_stage(t - 1)
-
-            return 0
-
-        lax.fori_loop(0, 2, half, 0)
+        gather_stage(t)
+
+        @pl.when((t >= 1) & (t <= heads))
+        def _():
+            compute_stage(t - 1)
+
+        sums(t - 2, True)
 
         @pl.when(t >= 3)
         def _():

time: 104 us -> 101 us (0.971)
  Pallas kernels: 96.6 us -> 93.5 us
    pallas_call x1, Pallas kernels: 96.6 us -> 93.5 us  [shards(): pl.pallas_call(functools.partial(kernel, nz, nx, nb, per, cap, heads), ou...]
where the time goes in v3:
time: 101 us
  Pallas kernels  93.5 us (93%)
  local copies, waits for them, and re-layouts  5.87 us (6%)
  between operations  1.3 us (1%)
    pallas_call x1, Pallas kernels, shards(): pl.pallas_call(functools.partial(kernel, nz, nx, nb, per, cap, heads), ou...  93.5 us
    unnamed x11, local copies, waits for them, and re-layouts  5.87 us

profile of v3, /device:TPU:0, one launch (start us, length us, event | category | flops | bytes accessed | tf_op | source)
XLA Modules:
  0.0 100.7 jit_solution(17981990317493260072)
XLA Ops:
  1.3 1.4 %copy.10.rb_ref = s32[32,3]{1,0:T(8,128)} copy(s32[32,3]{0,1:T(4,128)} %param.10) | data formatting | bytes 768 | tf_op args[4]
  2.6 93.5 %shard_map.93 = (bf16[256,512]{1,0:T(8,128)(2,1)}, bf16[256,512]{1,0:T(8,128)(2,1)}, bf16[256,512]{1,0:T(8,128)(2,1)}, bf16[256,512]{1,0:T(8,128)(2,1)}) custom-call(s32[32,3]{1,0:T(8,128)} %copy.10.rb_ref, s32[1]{0:T(128)S(6)} %copy.15.gb_ref, bf16[256,512]{1,0:T(8,128)(2,1)} %q_ref.1, bf16[256,512]{1,0:T(8,128)(2,1)} %k_ref.1, bf16[256,512]{1,0:T(8,128)(2,1)} %v_ref.1, ...), custom_call_target="tpu_custom_call" | custom-call | tf_op jit(solution)/shard_map/pallas_call | solution.py:567
  96.2 0.0 copy-start.2
  96.2 1.7 %copy.16 = bf16[256,512]{1,0:T(8,128)(2,1)} copy(bf16[256,512]{1,0:T(8,128)(2,1)} %get-tuple-element.8) | data formatting | bytes 524288
  97.9 0.0 copy-done.2
  97.9 0.0 copy-start.1
  97.9 0.7 copy.17
  98.6 0.3 copy-done.1
  99.0 0.0 copy-start
  99.0 0.7 copy.18
  99.7 0.3 copy-done
  100.0 0.7 copy.19
Async XLA Ops:
  96.2 1.7 %copy-start.2 = (bf16[256,512]{1,0:T(8,128)(2,1)S(1)}, bf16[256,512]{1,0:T(8,128)(2,1)}, u32[]{:S(2)}) copy-start(bf16[256,512]{1,0:T(8,128)(2,1)} %get-tuple-element.9) | copy-start | bytes 786436
  97.9 1.0 %copy-start.1 = (bf16[256,512]{1,0:T(8,128)(2,1)S(1)}, bf16[256,512]{1,0:T(8,128)(2,1)}, u32[]{:S(2)}) copy-start(bf16[256,512]{1,0:T(8,128)(2,1)} %get-tuple-element.10) | copy-start | bytes 786436
  99.0 1.0 %copy-start = (bf16[256,512]{1,0:T(8,128)(2,1)S(1)}, bf16[256,512]{1,0:T(8,128)(2,1)}, u32[]{:S(2)}) copy-start(bf16[256,512]{1,0:T(8,128)(2,1)} %get-tuple-element.11) | copy-start | bytes 786436
